TPU v7x, 32 devices: a whole 2x2x4 slice. The times are simulated.
32 devices in a mesh: fsdp: 4 (over z), seq: 8 (over y, x, core).
Axes of the slice: x: 2, y: 2, z: 4, core: 2. Of those that a mesh axis runs over, the one named last changes fastest.
Arguments:
- block_in: bfloat16 [3, 16384, 1280], P(None, ('fsdp', 'seq')), may hold values from -6 to 6
- cotangent: bfloat16 [3, 16384, 1280], P(None, ('fsdp', 'seq')), may hold values from -6 to 6
- lengths: int32 [3, 4, 8], P(None, 'fsdp'), may hold values from 1 to 4089, as said below
- item_weights: int32 [3, 4, 8], P(None, 'fsdp'), may hold values from 1 to 4
- first_gain: bfloat16 [1280], P('fsdp'), may hold values from 0.5 to 1.5
- first_shift: bfloat16 [1280], P('fsdp'), may hold values from -3 to 3
- entry_weight: bfloat16 [1280, 1280], P('fsdp'), may hold values from -0.15625 to 0.15625
- entry_bias: bfloat16 [1280], P('fsdp'), may hold values from -3 to 3
- middle_gain: bfloat16 [1280], P('fsdp'), may hold values from 0.5 to 1.5
- middle_shift: bfloat16 [1280], P('fsdp'), may hold values from -3 to 3
- conv_weight: bfloat16 [5, 1280, 1280], P(None, 'fsdp'), may hold values from -0.078125 to 0.078125
- conv_bias: bfloat16 [1280], P('fsdp'), may hold values from -3 to 3
- final_gain: bfloat16 [1280], P('fsdp'), may hold values from 0.5 to 1.5
- final_shift: bfloat16 [1280], P('fsdp'), may hold values from -3 to 3
- exit_weight: bfloat16 [1280, 1280], P(None, 'fsdp'), may hold values from -0.15625 to 0.15625
- exit_bias: bfloat16 [1280], P('fsdp'), may hold values from -3 to 3
Outputs:
- block_out: bfloat16 [3, 16384, 1280], P(None, ('fsdp', 'seq'))
- input_grad: bfloat16 [3, 16384, 1280], P(None, ('fsdp', 'seq'))
- first_gain_grad: float32 [1280], P('fsdp')
- first_shift_grad: float32 [1280], P('fsdp')
- entry_weight_grad: float32 [1280, 1280], P('fsdp')
- entry_bias_grad: float32 [1280], P('fsdp')
- middle_gain_grad: float32 [1280], P('fsdp')
- middle_shift_grad: float32 [1280], P('fsdp')
- conv_weight_grad: float32 [5, 1280, 1280], P(None, 'fsdp')
- conv_bias_grad: float32 [1280], P('fsdp')
- final_gain_grad: float32 [1280], P('fsdp')
- final_shift_grad: float32 [1280], P('fsdp')
- exit_weight_grad: float32 [1280, 1280], P(None, 'fsdp')
- exit_bias_grad: float32 [1280], P('fsdp')
Inputs may be any that keep to these rules, and one draw needn't show every extreme that they name: For each micro-batch and group the 8 lengths sum to at most 4096, the residues past their sum being padding; one item of each group, at a place drawn from the seed, is longer than 3584 and starts within the first 512 residues; in some group the other items have length 1 and there is no padding.
All inputs are finite; a program needn't handle non-finite values.
Results may differ from a plain program's by a relative error of at most 0.0072.
Values may be sent and summed in bfloat16 or wider, within the bound.
A program may use at most 256 MiB of HBM per device.

v0:
```python
import jax
import jax.numpy as jnp
from jax import lax
from jax.sharding import PartitionSpec as P

KERNEL_TAPS = 5
DILATION_STEP = 128


eps_norm = 1e-05


def norm_act(values, scale_vec, shift_vec):
    row_mean = jnp.mean(values, axis=-1, keepdims=True)
    centred = values - row_mean
    spread = jnp.mean(centred * centred, axis=-1, keepdims=True)
    return jax.nn.gelu(
        centred * lax.rsqrt(spread + eps_norm) * scale_vec + shift_vec, approximate=False
    )


def column_product(left, right):
    return lax.dot_general(
        left, right, (((0,), (0,)), ((), ())), preferred_element_type=jnp.float32
    )


def row_product(left, right):
    return lax.dot_general(
        left, right, (((1,), (1,)), ((), ())), preferred_element_type=jnp.float32
    )


def items_at(residue_position, item_lengths, stream_len):
    ends = jnp.cumsum(item_lengths)
    inside = (residue_position >= 0) & (residue_position < stream_len)
    seg_all = jnp.sum((residue_position[:, None] >= ends[None, :]).astype(jnp.int32), axis=1)
    return jnp.where(inside, seg_all, -1)


def stacked(extended, segment_extended, tap_offset, row_count, item_count):
    half_reach = KERNEL_TAPS // 2
    middle_tap = segment_extended[half_reach * tap_offset : half_reach * tap_offset + row_count]
    tap_parts = []
    for kernel_tap_index in range(KERNEL_TAPS):
        segment_tapped = segment_extended[
            kernel_tap_index * tap_offset : kernel_tap_index * tap_offset + row_count
        ]
        keep_mask = (
            (segment_tapped == middle_tap) & (segment_tapped >= 0) & (segment_tapped < item_count)
        )
        tap_parts.append(
            extended[kernel_tap_index * tap_offset : kernel_tap_index * tap_offset + row_count]
            * keep_mask[:, None].astype(extended.dtype)
        )
    return jnp.concatenate(tap_parts, axis=1)


def on_device(
    block_in,
    cotangent,
    lengths,
    item_weights,
    first_gain,
    first_shift,
    entry_weight,
    entry_bias,
    middle_gain,
    middle_shift,
    conv_weight,
    conv_bias,
    final_gain,
    final_shift,
    exit_weight,
    exit_bias,
):
    micro_count = block_in.shape[0]
    row_count = block_in.shape[1]
    model_width = block_in.shape[2]
    inner_width = entry_weight.shape[1]
    item_count = lengths.shape[2]
    sequence_count = lax.axis_size("seq")
    seq_place = lax.axis_index("seq")
    stream_len = row_count * sequence_count
    half_reach = KERNEL_TAPS // 2
    totals = [
        jnp.zeros((model_width,), jnp.float32),
        jnp.zeros((model_width,), jnp.float32),
        jnp.zeros((model_width, inner_width), jnp.float32),
        jnp.zeros((inner_width,), jnp.float32),
        jnp.zeros((inner_width,), jnp.float32),
        jnp.zeros((inner_width,), jnp.float32),
        jnp.zeros((KERNEL_TAPS, inner_width, inner_width), jnp.float32),
        jnp.zeros((inner_width,), jnp.float32),
        jnp.zeros((inner_width,), jnp.float32),
        jnp.zeros((inner_width,), jnp.float32),
        jnp.zeros((inner_width, model_width), jnp.float32),
        jnp.zeros((model_width,), jnp.float32),
    ]
    outputs = []
    input_grads = []
    for micro_index in range(micro_count):
        params = (
            lax.all_gather(first_gain, "fsdp", axis=0, tiled=True),
            lax.all_gather(first_shift, "fsdp", axis=0, tiled=True),
            lax.all_gather(entry_weight, "fsdp", axis=0, tiled=True),
            lax.all_gather(entry_bias, "fsdp", axis=0, tiled=True),
            lax.all_gather(middle_gain, "fsdp", axis=0, tiled=True),
            lax.all_gather(middle_shift, "fsdp", axis=0, tiled=True),
            lax.all_gather(conv_weight, "fsdp", axis=1, tiled=True),
            lax.all_gather(conv_bias, "fsdp", axis=0, tiled=True),
            lax.all_gather(final_gain, "fsdp", axis=0, tiled=True),
            lax.all_gather(final_shift, "fsdp", axis=0, tiled=True),
            lax.all_gather(exit_weight, "fsdp", axis=1, tiled=True),
            lax.all_gather(exit_bias, "fsdp", axis=0, tiled=True),
        )
        (
            gain_one,
            shift_one,
            weight_in,
            bias_in,
            gain_two,
            shift_two,
            weight_conv,
            bias_conv,
            gain_three,
            shift_three,
            weight_out,
            bias_out,
        ) = params
        item_lengths = lengths[micro_index, 0]
        weight_row = item_weights[micro_index, 0]
        own_position = seq_place * row_count + jnp.arange(row_count, dtype=jnp.int32)
        seg_own = items_at(own_position, item_lengths, stream_len)
        match = seg_own[:, None] == jnp.arange(item_count, dtype=jnp.int32)[None, :]
        row_scale = jnp.sum(jnp.where(match, weight_row[None, :], 0), axis=1).astype(jnp.float32)
        inputs = block_in[micro_index].astype(jnp.float32)
        normed_one, back_one = jax.vjp(
            norm_act, inputs, gain_one.astype(jnp.float32), shift_one.astype(jnp.float32)
        )
        act_one = normed_one.astype(jnp.bfloat16)
        inner_one = jnp.dot(
            act_one, weight_in, preferred_element_type=jnp.float32
        ) + bias_in.astype(jnp.float32)
        normed_two, back_two = jax.vjp(
            norm_act, inner_one, gain_two.astype(jnp.float32), shift_two.astype(jnp.float32)
        )
        second_activation = normed_two.astype(jnp.bfloat16)
        flat_conv = weight_conv.reshape(KERNEL_TAPS * inner_width, inner_width)
        flip_conv = (
            jnp.flip(weight_conv, 0)
            .transpose(0, 2, 1)
            .reshape(KERNEL_TAPS * inner_width, inner_width)
        )
        tap_offset = DILATION_STEP // sequence_count
        residue_position = (
            sequence_count
            * (
                jnp.arange(row_count + 2 * half_reach * tap_offset, dtype=jnp.int32)
                - half_reach * tap_offset
            )
            + seq_place
        )
        segment_extended = items_at(residue_position, item_lengths, stream_len)
        dealt = lax.all_to_all(
            second_activation.reshape(row_count // sequence_count, sequence_count, inner_width),
            "seq",
            split_axis=1,
            concat_axis=0,
            tiled=True,
        ).reshape(row_count, inner_width)
        extended = jnp.pad(dealt, ((half_reach * tap_offset, half_reach * tap_offset), (0, 0)))
        shifted_tap_rows = stacked(extended, segment_extended, tap_offset, row_count, item_count)
        dealt_out = (
            jnp.dot(shifted_tap_rows, flat_conv, preferred_element_type=jnp.float32)
            + bias_conv.astype(jnp.float32)
        ).astype(jnp.bfloat16)
        inner_two = lax.all_to_all(
            dealt_out.reshape(sequence_count, row_count // sequence_count, 1, inner_width),
            "seq",
            split_axis=0,
            concat_axis=2,
            tiled=True,
        ).reshape(row_count, inner_width)
        normed_three, back_three = jax.vjp(
            norm_act,
            inner_two.astype(jnp.float32),
            gain_three.astype(jnp.float32),
            shift_three.astype(jnp.float32),
        )
        act_three = normed_three.astype(jnp.bfloat16)
        branch = jnp.dot(
            act_three, weight_out, preferred_element_type=jnp.float32
        ) + bias_out.astype(jnp.float32)
        outputs.append((inputs + branch).astype(jnp.bfloat16))
        pulled = cotangent[micro_index].astype(jnp.float32) * row_scale[:, None]
        grad_branch = pulled.astype(jnp.bfloat16)
        sum_exit_weight = column_product(act_three, grad_branch)
        sum_exit_bias = jnp.sum(grad_branch.astype(jnp.float32), axis=0)
        grad_act_three = row_product(grad_branch, weight_out)
        grad_inner_two, sum_final_gain, sum_final_shift = back_three(grad_act_three)
        low_inner_two = grad_inner_two.astype(jnp.bfloat16)
        sum_conv_bias = jnp.sum(low_inner_two.astype(jnp.float32), axis=0)
        grad_dealt = lax.all_to_all(
            low_inner_two.reshape(row_count // sequence_count, sequence_count, inner_width),
            "seq",
            split_axis=1,
            concat_axis=0,
            tiled=True,
        ).reshape(row_count, inner_width)
        sum_conv_weight = column_product(shifted_tap_rows, grad_dealt)
        grad_ext = jnp.pad(grad_dealt, ((half_reach * tap_offset, half_reach * tap_offset), (0, 0)))
        dealt_back = jnp.dot(
            stacked(grad_ext, segment_extended, tap_offset, row_count, item_count),
            flip_conv,
            preferred_element_type=jnp.float32,
        )
        grad_act_two = lax.all_to_all(
            dealt_back.reshape(sequence_count, row_count // sequence_count, 1, inner_width),
            "seq",
            split_axis=0,
            concat_axis=2,
            tiled=True,
        ).reshape(row_count, inner_width)
        grad_inner_one, sum_middle_gain, sum_middle_shift = back_two(grad_act_two)
        low_inner_one = grad_inner_one.astype(jnp.bfloat16)
        sum_entry_weight = column_product(act_one, low_inner_one)
        sum_entry_bias = jnp.sum(low_inner_one.astype(jnp.float32), axis=0)
        grad_act_one = row_product(low_inner_one, weight_in)
        grad_inputs, sum_first_gain, sum_first_shift = back_one(grad_act_one)
        input_grads.append((pulled + grad_inputs).astype(jnp.bfloat16))
        fresh = (
            sum_first_gain,
            sum_first_shift,
            sum_entry_weight,
            sum_entry_bias,
            sum_middle_gain,
            sum_middle_shift,
            sum_conv_weight.reshape(KERNEL_TAPS, inner_width, inner_width),
            sum_conv_bias,
            sum_final_gain,
            sum_final_shift,
            sum_exit_weight,
            sum_exit_bias,
        )
        totals = [left + right for left, right in zip(totals, fresh)]
    shares = (
        lax.psum_scatter(totals[0], "fsdp", scatter_dimension=0, tiled=True),
        lax.psum_scatter(totals[1], "fsdp", scatter_dimension=0, tiled=True),
        lax.psum_scatter(totals[2], "fsdp", scatter_dimension=0, tiled=True),
        lax.psum_scatter(totals[3], "fsdp", scatter_dimension=0, tiled=True),
        lax.psum_scatter(totals[4], "fsdp", scatter_dimension=0, tiled=True),
        lax.psum_scatter(totals[5], "fsdp", scatter_dimension=0, tiled=True),
        lax.psum_scatter(totals[6], "fsdp", scatter_dimension=1, tiled=True),
        lax.psum_scatter(totals[7], "fsdp", scatter_dimension=0, tiled=True),
        lax.psum_scatter(totals[8], "fsdp", scatter_dimension=0, tiled=True),
        lax.psum_scatter(totals[9], "fsdp", scatter_dimension=0, tiled=True),
        lax.psum_scatter(totals[10], "fsdp", scatter_dimension=1, tiled=True),
        lax.psum_scatter(totals[11], "fsdp", scatter_dimension=0, tiled=True),
    )
    result = lax.psum(
        (
            shares[0],
            shares[1],
            shares[2],
            shares[3],
            shares[4],
            shares[5],
            shares[6],
            shares[7],
            shares[8],
            shares[9],
            shares[10],
            shares[11],
        ),
        "seq",
    )
    return (
        jnp.stack(outputs),
        jnp.stack(input_grads),
        result[0],
        result[1],
        result[2],
        result[3],
        result[4],
        result[5],
        result[6],
        result[7],
        result[8],
        result[9],
        result[10],
        result[11],
    )


def solution(mesh):
    in_specs = (
        P(None, ("fsdp", "seq"), None),
        P(None, ("fsdp", "seq"), None),
        P(None, "fsdp", None),
        P(None, "fsdp", None),
        P("fsdp"),
        P("fsdp"),
        P("fsdp", None),
        P("fsdp"),
        P("fsdp"),
        P("fsdp"),
        P(None, "fsdp", None),
        P("fsdp"),
        P("fsdp"),
        P("fsdp"),
        P(None, "fsdp"),
        P("fsdp"),
    )
    out_specs = (
        P(None, ("fsdp", "seq"), None),
        P(None, ("fsdp", "seq"), None),
        P("fsdp"),
        P("fsdp"),
        P("fsdp", None),
        P("fsdp"),
        P("fsdp"),
        P("fsdp"),
        P(None, "fsdp", None),
        P("fsdp"),
        P("fsdp"),
        P("fsdp"),
        P(None, "fsdp"),
        P("fsdp"),
    )
    return jax.shard_map(
        on_device, mesh=mesh, in_specs=in_specs, out_specs=out_specs, check_vma=False
    )
```

profile of v0, /device:TPU:0, one launch (start us, length us, event | category | flops | bytes accessed | tf_op | source)
XLA Modules:
  0.0 1601.7 jit_solution(953524988109380144)
XLA Ops:
  13.1 23.4 %all-reduce.27 = (bf16[1280]{0:T(1024)(128)(2,1)S(1)}, bf16[1280]{0:T(1024)(128)(2,1)S(1)}, bf16[1280]{0:T(1024)(128)(2,1)S(1)}, bf16[1280]{0:T(1024)(128)(2,1)S...) all-reduce(bf16[1280]{0:T(1024)(128)(2,1)S(1)} %dynamic-update-slic, ...), channel_id=1, replica_groups=mesh['fsdp'=4,'seq'=8] {'fsdp'}, use_global_device_ids=true, to_apply=%add.7 | all-reduce | flops 11520 | bytes 46080
  42.9 21.5 %multiply_convert_fusion.8 = (bf16[512,1280]{1,0:T(8,128)(2,1)}, f32[512,1280]{1,0:T(8,128)}, bf16[512,1280]{1,0:T(8,128)(2,1)S(1)}, f32[512,1280]{1,0:T(8,128)}...) fusion(f32[1280]{0:T(1024)S(1)} %convert_element_type.409, f32[1280]{0:T(1024)S(1)} %convert_element_type.408, ...), kind=kLoop, calls=%fused_computation.411 | loop fusion | flops 137625600 | bytes 15751168 | tf_op jit(solution)/shard_map/convert_element_type | solution.py:141
  64.4 14.5 all-gather.4.cloned.1.call-done
  88.9 20.5 %fusion.243 = (bf16[64,8,1280]{2,1,0:T(8,128)(2,1)S(1)}, f32[512,1280]{1,0:T(8,128)}, bf16[64,8,1280]{2,1,0:T(8,128)(2,1)}, f32[512,1280]{1,0:T(8,128)}, bf16[64...) fusion(f32[512,1280]{1,0:T(8,128)S(1)} %get-tuple-element.208, f32[1280]{0:T(1024)S(1)} %convert_element_type.413, ...), kind=kLoop, calls=%fused_computation.435 | loop fusion | flops 135659520 | bytes 19683328 | tf_op jit(solution)/shard_map/reshape | solution.py:166
  118.8 13.8 all-to-all-done
  190.4 169.2 %all-gather.6.cloned.1.call-done = bf16[5,1280,1280]{2,1,0:T(8,128)(2,1)} async-done(((bf16[5,320,1280]{2,1,0:T(8,128)(2,1)}), bf16[5,1280,1280]{2,1,0:T(8,128)(2,1)}) %all-gather.6.cloned.1.call-update) | async-done | bytes 16384016 | tf_op jit(solution)/shard_map/all_gather | solution.py:110
  359.6 14.6 fusion.33
  378.3 14.7 fusion.34
  393.0 14.7 fusion.35
  425.6 21.9 %copy.139 = bf16[5,1280,1280]{2,1,0:T(8,128)(2,1)} copy(bf16[5,1280,1280]{1,2,0:T(8,128)(2,1)} %reverse_bitcast_fusion) | data formatting | bytes 32768000 | tf_op jit(solution)/shard_map/transpose | solution.py:152
  455.5 15.4 all-to-all-done.5
  475.4 22.2 %fusion.143 = (f32[512,1280]{1,0:T(8,128)}, f32[512,1280]{1,0:T(8,128)}, f32[512,1280]{1,0:T(8,128)}) fusion(f32[1280]{0:T(1024)S(1)} %convert_element_type.429, f32[1280]{0:T(1024)S(1)} %convert_element_type.428, f32[512]{0:T(512)S(1)} %rsqrt.101, f32[512]{0:T(512)S(1)} %div.173, bf16[8,64,1,1280]{3,1,2,0:T(8,128)(2,1)S(1)} %all-to-all-done.1, ...), kind=kLoop, calls=%fused_computation.203 | loop fusion | flops 131727360 | bytes 11819008 | tf_op jit(solution)/shard_map/jvp()/erfc | solution.py:17
  597.8 17.9 %convolution_bitcast_fusion = f32[8,64,1,1280]{3,1,2,0:T(8,128)} fusion(bf16[8,64,6400]{2,1,0:T(8,128)(2,1)} %bitcast.92, bf16[6400,1280,1]{1,0,2:T(8,128)(2,1)} %bitcast.770), kind=kOutput, calls=%fused_computation.81 | convolution fusion | flops 8388608000 | bytes 25559040 | tf_op jit(solution)/shard_map/dot_general | solution.py:213
  637.6 25.2 %all-to-all-done.11 = f32[8,64,1,1280]{3,1,2,0:T(8,128)} async-done(((f32[8,64,1,1280]{3,1,2,0:T(8,128)}), f32[8,64,1,1280]{3,1,2,0:T(8,128)}, u32[]{:S(2)}, u32[]{:S(2)}) %all-to-all-start.11) | async-done | bytes 2621472 | tf_op jit(solution)/shard_map/all_to_all | solution.py:218
  667.3 15.0 convolution_bitcast_fusion.2
  682.3 17.1 %all-to-all-done.9 = f32[8,64,1,1280]{3,1,2,0:T(8,128)} async-done(((f32[8,64,1,1280]{3,1,2,0:T(8,128)}), f32[8,64,1,1280]{3,1,2,0:T(8,128)}, u32[]{:S(2)}, u32[]{:S(2)}) %all-to-all-start.9) | async-done | bytes 2621472 | tf_op jit(solution)/shard_map/all_to_all | solution.py:218
  699.4 36.1 %all_to_all.162 = f32[8,64,1,1280]{3,1,2,0:T(8,128)S(1)} all-to-all(f32[8,64,1,1280]{3,1,2,0:T(8,128)} %convolution_bitcast_fusion.2), channel_id=1, replica_groups=mesh['fsdp'=4,'seq'=8] {'seq'}, dimensions={0} | all-to-all | bytes 5242880 | tf_op jit(solution)/shard_map/all_to_all | solution.py:218
  790.9 19.4 %fusion.539 = f32[5,1280,1280]{2,1,0:T(8,128)} fusion(bf16[5,1280,512]{2,1,0:T(8,128)(2,1)} %bitcast.754, bf16[512,1280,1]{1,0,2:T(8,128)(2,1)S(1)} %bitcast.741), kind=kOutput, calls=%fused_computation.825 | convolution fusion | flops 8388608000 | bytes 40632320 | tf_op jit(solution)/shard_map/dot_general | solution.py:23
  810.3 28.2 %convolution_add_fusion.1 = f32[5,1280,1280]{2,1,0:T(8,128)} fusion(f32[5,1280,1280]{2,1,0:T(8,128)} %fusion.539, bf16[5,1280,512]{2,1,0:T(8,128)(2,1)} %bitcast.766, bf16[512,1280,1]{1,0,2:T(8,128)(2,1)S(1)} %bitcast.753), kind=kOutput, calls=%fused_computation.1 | convolution fusion | flops 8396800000 | bytes 73400320 | tf_op jit(solution)/shard_map/dot_general | solution.py:23
  838.5 28.2 %convolution_add_fusion = f32[5,1280,1280]{2,1,0:T(8,128)} fusion(f32[5,1280,1280]{2,1,0:T(8,128)} %convolution_add_fusion.1, bf16[5,1280,512]{2,1,0:T(8,128)(2,1)} %bitcast.765, bf16[512,1280,1]{1,0,2:T(8,128)(2,1)S(1)} %bitcast.747), kind=kOutput, calls=%fused_computation | convolution fusion | flops 8396800000 | bytes 73400320 | tf_op jit(solution)/shard_map/dot_general | solution.py:23
  891.1 525.0 %reduce-scatter.6.cloned.1.call-done = f32[5,320,1280]{2,1,0:T(8,128)} async-done(((f32[5,1280,1280]{2,1,0:T(8,128)}), f32[5,320,1280]{2,1,0:T(8,128)}) %reduce-scatter.6.cloned.1.call-update) | async-done | bytes 8192016 | tf_op jit(solution)/shard_map/reduce_scatter | solution.py:254
  1437.2 19.6 %all-reduce.26 = (f32[1280]{0:T(1024)S(1)}, f32[1280]{0:T(1024)S(1)}, f32[1280]{0:T(1024)S(1)}, f32[1280]{0:T(1024)S(1)}, f32[1280]{0:T(1024)S(1)}, /*index=5*/f...) all-reduce(f32[1280]{0:T(1024)S(1)} %add_add_fusion.17, ...), channel_id=2, replica_groups=mesh['fsdp'=4,'seq'=8] {'fsdp'}, use_global_device_ids=true, to_apply=%region_51.52.clone | all-reduce | flops 11520 | bytes 92160
  1457.5 24.3 %all-reduce.24 = (f32[320]{0:T(512)}, f32[320]{0:T(512)}, f32[320]{0:T(512)}, f32[320]{0:T(512)}, f32[320]{0:T(512)}, /*index=5*/f32[320]{0:T(512)}, f32[320]{0:T(512)}, f32[320]{0:T(512)}, f32[320]{0:T(512)}) all-reduce(f32[320]{0:T(512)S(1)} %dynamic-slice.10, ...), channel_id=1, replica_groups=mesh['fsdp'=4,'seq'=8] {'seq'}, use_global_device_ids=true, to_apply=%region_52.53 | all-reduce | flops 2880 | bytes 23040 | tf_op jit(solution)/shard_map/psum | solution.py:261
  1485.2 97.9 %all-reduce.30.cloned.1.call-done = (f32[320,1280]{1,0:T(8,128)}, f32[5,320,1280]{2,1,0:T(8,128)}, f32[1280,320]{0,1:T(8,128)}) async-done(((f32[320,1280]{1,0:T(8,128)}, f32[5,320,1280]{2,1,0:T(8,128)}, f32[1280,320]{0,1:T(8,128)}), (f32[320,1280]{1,0:T(8,128)}, f32[5,320,1280]{2,1,0:T(8,128)}, f32[1280,320]{0,1:T(8,128)})) %all-reduce.30.cloned.1.call-update) | async-done | bytes 11468816 | tf_op jit(solution)/shard_map/psum | solution.py:261
  (562 shorter events, 362.9 us)
Async XLA Ops:
  7.2 71.8 %all-gather.4.cloned.1.call-start = ((), (), s32[]{:S(2)}) async-start(), calls=%async_computation.15 | async-start | bytes 4096000 | tf_op jit(solution)/shard_map/all_gather | solution.py:106
  8.0 351.6 %all-gather.6.cloned.1.call-start = ((), (), s32[]{:S(2)}) async-start(), calls=%async_computation.16 | async-start | bytes 20480000 | tf_op jit(solution)/shard_map/all_gather | solution.py:110
  8.8 488.8 %all-gather.8.cloned.1.call-start = ((), (), s32[]{:S(2)}) async-start(), calls=%async_computation.17 | async-start | bytes 4096000 | tf_op jit(solution)/shard_map/all_gather | solution.py:114
  110.7 21.9 %all-to-all-start = ((bf16[64,8,1280]{2,0,1:T(8,128)(2,1)}), bf16[64,8,1280]{2,0,1:T(8,128)(2,1)S(1)}, u32[]{:S(2)}, u32[]{:S(2)}) async-start(bf16[64,8,1280]{2,0,1:T(8,128)(2,1)} %copy.129), calls=%async_computation | async-start | bytes 2621440 | tf_op jit(solution)/shard_map/all_to_all | solution.py:165
  114.5 440.6 %copy-start.66 = (f32[1280]{0:T(1024)}, f32[1280]{0:T(1024)S(1)}, u32[]{:S(2)}) copy-start(f32[1280]{0:T(1024)S(1)} %convert_element_type.429) | copy-start | bytes 15364
  114.5 440.6 %copy-start.42 = (f32[1280]{0:T(1024)}, f32[1280]{0:T(1024)S(1)}, u32[]{:S(2)}) copy-start(f32[1280]{0:T(1024)S(1)} %convert_element_type.428) | copy-start | bytes 15364
  114.5 432.2 %copy-start.131 = (f32[512]{0:T(512)}, f32[512]{0:T(512)S(1)}, u32[]{:S(2)}) copy-start(f32[512]{0:T(512)S(1)} %convert_element_type.480) | copy-start | bytes 6148
  114.5 424.1 %copy-start.133 = (f32[512]{0:T(512)}, f32[512]{0:T(512)S(1)}, u32[]{:S(2)}) copy-start(f32[512]{0:T(512)S(1)} %convert_element_type.472) | copy-start | bytes 6148
  114.6 440.5 %copy-start.135 = (f32[512]{0:T(512)}, f32[512]{0:T(512)S(1)}, u32[]{:S(2)}) copy-start(f32[512]{0:T(512)S(1)} %convert_element_type.488) | copy-start | bytes 6148
  132.6 21.7 %all-to-all-start.2 = ((bf16[64,8,1280]{2,0,1:T(8,128)(2,1)}), bf16[64,8,1280]{2,0,1:T(8,128)(2,1)S(1)}, u32[]{:S(2)}, u32[]{:S(2)}) async-start(bf16[64,8,1280]{2,0,1:T(8,128)(2,1)} %copy.132), calls=%async_computation.2 | async-start | bytes 2621440 | tf_op jit(solution)/shard_map/all_to_all | solution.py:165
  154.3 22.5 %all-to-all-start.4 = ((bf16[64,8,1280]{2,0,1:T(8,128)(2,1)}), bf16[64,8,1280]{2,0,1:T(8,128)(2,1)}, u32[]{:S(2)}, u32[]{:S(2)}) async-start(bf16[64,8,1280]{2,0,1:T(8,128)(2,1)} %copy.135), calls=%async_computation.4 | async-start | bytes 2621440 | tf_op jit(solution)/shard_map/all_to_all | solution.py:165
  374.2 33.5 %all-to-all-start.1 = ((bf16[8,64,1,1280]{3,1,2,0:T(8,128)(2,1)}), bf16[8,64,1,1280]{3,1,2,0:T(8,128)(2,1)S(1)}, u32[]{:S(2)}, u32[]{:S(2)}) async-start(bf16[8,64,1,1280]{3,1,2,0:T(8,128)(2,1)} %bitcast.12), calls=%async_computation.1 | async-start | bytes 2621440 | tf_op jit(solution)/shard_map/all_to_all | solution.py:178
  407.8 130.8 %copy-start.12 = (bf16[8,64,1,1280]{3,1,2,0:T(8,128)(2,1)}, bf16[8,64,1,1280]{3,1,2,0:T(8,128)(2,1)S(1)}, u32[]{:S(2)}) copy-start(bf16[8,64,1,1280]{3,1,2,0:T(8,128)(2,1)S(1)} %all-to-all-done.1) | copy-start | bytes 3932164
  407.8 40.5 %all-to-all-start.3 = ((bf16[8,64,1,1280]{3,1,2,0:T(8,128)(2,1)}), bf16[8,64,1,1280]{3,1,2,0:T(8,128)(2,1)S(1)}, u32[]{:S(2)}, u32[]{:S(2)}) async-start(bf16[8,64,1,1280]{3,1,2,0:T(8,128)(2,1)} %bitcast.777), calls=%async_computation.3 | async-start | bytes 2621440 | tf_op jit(solution)/shard_map/all_to_all | solution.py:178
  448.3 22.7 %all-to-all-start.5 = ((bf16[8,64,1,1280]{3,1,2,0:T(8,128)(2,1)}), bf16[8,64,1,1280]{3,1,2,0:T(8,128)(2,1)}, u32[]{:S(2)}, u32[]{:S(2)}) async-start(bf16[8,64,1,1280]{3,1,2,0:T(8,128)(2,1)} %bitcast.776), calls=%async_computation.5 | async-start | bytes 2621440 | tf_op jit(solution)/shard_map/all_to_all | solution.py:178
  528.2 39.6 %all-to-all-start.10 = ((bf16[64,8,1280]{2,0,1:T(8,128)(2,1)}), bf16[64,8,1280]{2,0,1:T(8,128)(2,1)S(1)}, u32[]{:S(2)}, u32[]{:S(2)}) async-start(bf16[64,8,1280]{2,0,1:T(8,128)(2,1)} %copy.145), calls=%async_computation.10 | async-start | bytes 2621440 | tf_op jit(solution)/shard_map/all_to_all | solution.py:204
  531.8 359.3 %reduce-scatter.8.cloned.1.call-start = ((), (), s32[]{:S(2)}) async-start(), calls=%async_computation.20 | async-start | bytes 8192000 | tf_op jit(solution)/shard_map/reduce_scatter | solution.py:258
  567.8 22.3 %all-to-all-start.8 = ((bf16[64,8,1280]{2,0,1:T(8,128)(2,1)}), bf16[64,8,1280]{2,0,1:T(8,128)(2,1)S(1)}, u32[]{:S(2)}, u32[]{:S(2)}) async-start(bf16[64,8,1280]{2,0,1:T(8,128)(2,1)} %copy.142), calls=%async_computation.8 | async-start | bytes 2621440 | tf_op jit(solution)/shard_map/all_to_all | solution.py:204
  591.2 34.7 %all-to-all-start.6 = ((bf16[64,8,1280]{2,0,1:T(8,128)(2,1)}), bf16[64,8,1280]{2,0,1:T(8,128)(2,1)S(1)}, u32[]{:S(2)}, u32[]{:S(2)}) async-start(bf16[64,8,1280]{2,0,1:T(8,128)(2,1)} %copy.138), calls=%async_computation.6 | async-start | bytes 2621440 | tf_op jit(solution)/shard_map/all_to_all | solution.py:204
  625.9 36.9 %all-to-all-start.11 = ((f32[8,64,1,1280]{3,1,2,0:T(8,128)}), f32[8,64,1,1280]{3,1,2,0:T(8,128)}, u32[]{:S(2)}, u32[]{:S(2)}) async-start(f32[8,64,1,1280]{3,1,2,0:T(8,128)} %convolution_bitcast_fusion), calls=%async_computation.11 | async-start | bytes 5242880 | tf_op jit(solution)/shard_map/all_to_all | solution.py:218
  662.8 36.7 %all-to-all-start.9 = ((f32[8,64,1,1280]{3,1,2,0:T(8,128)}), f32[8,64,1,1280]{3,1,2,0:T(8,128)}, u32[]{:S(2)}, u32[]{:S(2)}) async-start(f32[8,64,1,1280]{3,1,2,0:T(8,128)} %convolution_bitcast_fusion.1), calls=%async_computation.9 | async-start | bytes 5242880 | tf_op jit(solution)/shard_map/all_to_all | solution.py:218
  667.2 224.0 %reduce-scatter.4.cloned.1.call-start = ((), (), s32[]{:S(2)}) async-start(), calls=%async_computation.18 | async-start | bytes 8192000 | tf_op jit(solution)/shard_map/reduce_scatter | solution.py:250
  762.3 653.8 %reduce-scatter.6.cloned.1.call-start = ((), (), s32[]{:S(2)}) async-start(), calls=%async_computation.19 | async-start | bytes 40960000 | tf_op jit(solution)/shard_map/reduce_scatter | solution.py:254
  866.8 716.4 %all-reduce.30.cloned.1.call-start = ((), (), s32[]{:S(2)}) async-start(), calls=%async_computation.21 | async-start | bytes 22937600 | tf_op jit(solution)/shard_map/psum | solution.py:261
  (158 other events, 2606.0 us)
Sparse Core Ops, SparseCore 0:
  9.6 69.3 all-gather.3
  80.6 278.9 all-gather.5
  361.1 63.8 all-gather.7
  567.9 113.6 reduce-scatter.7
  762.4 111.4 reduce-scatter.3
  876.1 539.9 reduce-scatter.5
  1420.6 162.4 all-reduce.29
where the time goes:
time: 1610 us; the launch traced here: 1600 us
  waiting for transfers between devices  914 us (57%)
  matrix products  259 us (16%)
  other arithmetic  163 us (10%)
  blocking collectives  104 us (6%)
  local copies, waits for them, and re-layouts  97.4 us (6%)
  starting transfers between devices  45.8 us (3%)
  between operations  18.3 us (1%)
    reduce_scatter x1, waiting for transfers between devices, on_device(): lax.psum_scatter(totals[6], 'fsdp', scatter_dimension=1, tiled=True)  525 us
    all_gather x1, waiting for transfers between devices, on_device(): lax.all_gather(conv_weight, 'fsdp', axis=1, tiled=True)  169 us
    dot_general x9, matrix products, column_product(): lax.dot_general(left, right, (((0,), (0,)), ((), ())), preferred_element_...  113 us
    psum x1, waiting for transfers between devices, on_device(): lax.psum((shares[0], shares[1], shares[2], shares[3], shares[4], shares[5...  97.9 us
    dot_general x3, matrix products, on_device(): jnp.dot(shifted_tap_rows, flat_conv, preferred_element_type=jnp.float32)  44.1 us
    dot_general x3, matrix products, on_device(): jnp.dot(stacked(grad_ext, segment_extended, tap_offset, row_count, item_c...  43.1 us
    unnamed x2, blocking collectives  43 us
    all_to_all x2, waiting for transfers between devices, on_device(): lax.all_to_all(dealt_back.reshape(sequence_count, row_count // sequence_c...  42.3 us
  transfers between devices with their start and end apart: 18, of which 11 were waited for; matrix products, arithmetic and copies ran while one was open for 29% of the time, Pallas kernels for 0%

commit v1 on v0

--- a/solution.py
+++ b/solution.py
@@ -1,6 +1,11 @@
+import functools
+import math
+
 import jax
 import jax.numpy as jnp
 from jax import lax
+from jax.experimental import pallas as pl
+from jax.experimental.pallas import tpu as pltpu
 from jax.sharding import PartitionSpec as P
 
 KERNEL_TAPS = 5
@@ -8,6 +13,1076 @@
 
 
 eps_norm = 1e-05
+
+MESH = pl.DeviceIdType.MESH
+BF = jnp.bfloat16
+F32 = jnp.float32
+LANES = 128
+VMEM_MOST = 60 << 20
+NN = (((1,), (0,)), ((), ()))
+NT = (((1,), (1,)), ((), ()))
+TN = (((0,), (0,)), ((), ()))
+ROOT_HALF = math.sqrt(0.5)
+PHI_SCALE = 1.0 / math.sqrt(2.0 * math.pi)
+EXP2_SCALE = -0.5 * math.log2(math.e)
+G1, S1, BE, G2, S2, BC, G3, S3, BX = range(9)
+VECTORS = 16
+
+
+def mm(left, right, dims):
+    return lax.dot_general(left, right, dims, preferred_element_type=F32)
+
+
+def normed(v):
+    centred = v - jnp.mean(v, axis=-1, keepdims=True)
+    inverse = lax.rsqrt(jnp.mean(centred * centred, axis=-1, keepdims=True) + eps_norm)
+    return centred * inverse, inverse
+
+
+def phi(u):
+    return 0.5 + 0.5 * lax.erf(u * ROOT_HALF)
+
+
+def slope(u, big_phi):
+    return big_phi + u * (PHI_SCALE * jnp.exp2(u * u * EXP2_SCALE))
+
+
+def fold(tile):
+    return jnp.sum(tile.reshape(tile.shape[0] // 8, 8, tile.shape[1]), axis=0)
+
+
+def pull_back(t, n, inverse, gain):
+    at = t * gain
+    return (
+        at - jnp.mean(at, axis=-1, keepdims=True) - n * jnp.mean(at * n, axis=-1, keepdims=True)
+    ) * inverse
+
+
+def span(i, size):
+    return pl.ds(pl.multiple_of(i * size, size), size)
+
+
+def for_each(count, step):
+    lax.fori_loop(0, count, lambda i, carry: (step(i), carry)[1], 0)
+
+
+def wide(mask, width):
+    return jnp.concatenate([mask] * (width // LANES), axis=1)
+
+
+class Place:
+    def __init__(self):
+        self.z = lax.axis_index("fsdp")
+        self.s = lax.axis_index("seq")
+        self.nz = lax.axis_size("fsdp")
+        self.ns = lax.axis_size("seq")
+        s = self.s
+        self.c = lax.rem(s, 2)
+        self.x = lax.rem(s // 2, 2)
+        self.y = s // 4
+        self.q = s // 2
+        self.core = (self.z, s + 1 - 2 * self.c)
+        self.px = (self.z, s + 2 - 4 * self.x)
+        self.py = (self.z, s + 4 - 8 * self.y)
+        self.left = (self.z, lax.rem(s + self.ns - 1, self.ns))
+        self.right = (self.z, lax.rem(s + 1, self.ns))
+
+    def up(self, j):
+        return lax.rem(self.z + j, self.nz)
+
+    def down(self, j):
+        return lax.rem(self.z + self.nz - j, self.nz)
+
+    def above(self, j):
+        return (self.up(j), self.s)
+
+    def greet(self):
+        peers = [self.core, self.px, self.py, self.left, self.right]
+        peers += [self.above(j) for j in range(1, self.nz)]
+        barrier = pltpu.get_barrier_semaphore()
+        for peer in peers:
+            pl.semaphore_signal(barrier, inc=1, device_id=peer, device_id_type=MESH)
+        pl.semaphore_wait(barrier, len(peers))
+
+
+def send(src, dst, send_sem, recv_sem, peer):
+    return pltpu.make_async_remote_copy(
+        src_ref=src,
+        dst_ref=dst,
+        send_sem=send_sem,
+        recv_sem=recv_sem,
+        device_id=peer,
+        device_id_type=MESH,
+    )
+
+
+def find_items(place, lengths, weights, item, scale, micro, rows, halo):
+    extent = rows + 2 * halo
+    count = lengths.shape[1]
+    for m in range(micro):
+        position = lax.broadcasted_iota(jnp.int32, (extent, LANES), 0) + (place.s * rows - halo)
+        found = jnp.zeros((extent, LANES), jnp.int32)
+        end = jnp.int32(0)
+        ends = []
+        for j in range(count):
+            end = end + lengths[m, j]
+            ends.append(end)
+            found = found + jnp.where(position >= end, 1, 0)
+        found = jnp.where(
+            (position >= 0) & (position < place.ns * rows) & (found < count), found, -1
+        )
+        item[m] = found
+        if scale is not None:
+            own = found[halo : halo + rows]
+            total = jnp.zeros((rows, LANES), jnp.int32)
+            for j in range(count):
+                total = total + jnp.where(own == j, weights[m, j], 0)
+            scale[m] = total.astype(F32)
+
+
+def keep(item, m, tap, rows, halo):
+    own = item[m, halo : halo + rows]
+    first = pl.multiple_of(halo + (tap - KERNEL_TAPS // 2) * DILATION_STEP, DILATION_STEP)
+    other = item[m, pl.ds(first, rows)]
+    return jnp.where((own == other) & (own >= 0), 1.0, 0.0).astype(F32)
+
+
+TAP_ORDER = (2, 1, 3, 0, 4)
+
+
+def forward_kernel(
+    block_in, cotangent, lengths, weights, vectors, entry, conv, exit_t,
+    gathered, act_one, inner_one, ext_two, act_three, grad_two, grad_branch, params, sums,
+    held, total, grad_three, tap_w, one, pulled, item, scale, parts,
+    vec_send, vec_recv, z_send, z_recv, a_send, a_recv, b_send, b_recv, c_send, c_recv,
+    halo_send, halo_recv, load_sem, store_sem, tap_sem,
+):
+    place = Place()
+    micro, rows, width = block_in.shape
+    halo = (KERNEL_TAPS // 2) * DILATION_STEP
+    z, c, q, x, y, nz = place.z, place.c, place.q, place.x, place.y, place.nz
+    shard = entry.shape[0]
+    piece = shard // 4
+    half = width // 2
+    taps = conv.shape[0] + 2
+    order = [0, 1] + [2 + k for k in TAP_ORDER]
+    tile_n = 256
+    tile_r = 64
+    others = range(1, nz)
+
+    loads = []
+    for m in range(micro):
+        loads.append(pltpu.make_async_copy(block_in.at[m], one.at[m], load_sem.at[0, m]))
+        loads.append(pltpu.make_async_copy(cotangent.at[m], pulled.at[m], load_sem.at[1, m]))
+    for load in loads:
+        load.start()
+    own = []
+    for t in range(taps):
+        src = entry if t == 0 else exit_t if t == 1 else conv.at[t - 2]
+        own.append((src, pltpu.make_async_copy(src, gathered.at[t, pl.ds(z * shard, shard)], tap_sem.at[2, t])))
+    place.greet()
+
+    cols = pl.ds(pl.multiple_of(c * half, LANES), half)
+
+    def at(t, zz, first, count):
+        return gathered.at[t, pl.ds(zz * shard + first * piece, count * piece), cols]
+
+    vec_copies = [
+        send(vectors, parts.at[z], vec_send.at[j - 1], vec_recv.at[j - 1], place.above(j))
+        for j in others
+    ]
+    for copy in vec_copies:
+        copy.start()
+    parts[z] = vectors[...]
+
+    z_copies, a_copies, b_copies, c_copies = {}, {}, {}, {}
+
+    def spread_z(i):
+        t = order[i]
+        src = own[t][0]
+        for j in others:
+            copy = send(src.at[pl.ds(q * piece, piece), cols], at(t, z, q, 1), z_send.at[t, j - 1], z_recv.at[t, j - 1], place.above(j))
+            copy.start()
+            z_copies[t, j] = copy
+        own[t][1].start()
+
+    def first_axis(i):
+        return place.px if i % 2 == 0 else place.py
+
+    def spread_a(i):
+        t = order[i]
+        for j in others:
+            z_copies[t, j].wait_recv()
+            block = at(t, place.down(j), q, 1)
+            copy = send(block, block, a_send.at[t, j - 1], a_recv.at[t, j - 1], first_axis(i))
+            copy.start()
+            a_copies[t, j] = copy
+
+    def spread_b(i):
+        t = order[i]
+        for j in others:
+            a_copies[t, j].wait_recv()
+            zz = place.down(j)
+            if i % 2 == 0:
+                blocks = [at(t, zz, 2 * y, 2)]
+                peer = place.py
+            else:
+                blocks = [at(t, zz, x, 1), at(t, zz, x + 2, 1)]
+                peer = place.px
+            copies = []
+            for n, block in enumerate(blocks):
+                copy = send(block, block, b_send.at[t, j - 1, n], b_recv.at[t, j - 1, n], peer)
+                copy.start()
+                copies.append(copy)
+            b_copies[t, j] = copies
+
+    def spread_c(i):
+        t = order[i]
+        for j in others:
+            for copy in b_copies[t, j]:
+                copy.wait_recv()
+            block = at(t, place.down(j), 0, 4)
+            copy = send(block, block, c_send.at[t, j - 1], c_recv.at[t, j - 1], place.core)
+            copy.start()
+            c_copies[t, j] = copy
+
+    tap_loads = {}
+
+    def arrived(i):
+        t = order[i]
+        for j in others:
+            c_copies[t, j].wait_recv()
+        own[t][1].wait()
+        tap_loads[i] = pltpu.make_async_copy(gathered.at[t], tap_w.at[i % 2], tap_sem.at[i % 2, 0])
+        tap_loads[i].start()
+
+    def tick(i):
+        if i + 3 < taps:
+            spread_z(i + 3)
+        if i < taps:
+            spread_a(i)
+        if 0 <= i - 1 < taps:
+            spread_b(i - 1)
+        if 0 <= i - 2 < taps:
+            spread_c(i - 2)
+        if 0 <= i - 3 < taps:
+            arrived(i - 3)
+
+    for i in range(3):
+        spread_z(i)
+
+    find_items(place, lengths, weights, item, scale, micro, rows, halo)
+    for copy in vec_copies:
+        copy.wait_recv()
+    stacked_parts = [parts[zz].astype(F32)[:, :shard] for zz in range(nz)]
+    params[...] = jnp.concatenate(stacked_parts, axis=1)
+
+    def vec(r):
+        return params[r : r + 1, :]
+
+    sums[...] = jnp.zeros_like(sums)
+
+    def norm_one(m):
+        def step(i):
+            rs = span(i, tile_r)
+            n, _ = normed(one[m, rs, :].astype(F32))
+            u = n * vec(G1) + vec(S1)
+            one[m, rs, :] = (u * phi(u)).astype(BF)
+
+        for_each(rows // tile_r, step)
+
+    stores = []
+
+    def store(src, dst):
+        copy = pltpu.make_async_copy(src, dst, store_sem.at[len(stores)])
+        copy.start()
+        stores.append(copy)
+        return copy
+
+    one_out = []
+    for m in range(micro):
+        loads[2 * m].wait()
+        norm_one(m)
+        one_out.append(store(one.at[m], act_one.at[m]))
+    tick(0)
+
+    def pull(m):
+        def step(i):
+            rs = span(i, tile_r)
+            value = (pulled[m, rs, :].astype(F32) * wide(scale[m, rs, :], width)).astype(BF)
+            pulled[m, rs, :] = value
+            sums[3] += fold(value.astype(F32))
+
+        for_each(rows // tile_r, step)
+
+    branch_out = []
+    for m in range(micro):
+        loads[2 * m + 1].wait()
+        pull(m)
+        branch_out.append(store(pulled.at[m], grad_branch.at[m]))
+    tick(1)
+    tick(2)
+    tick(3)
+
+    def halo_right(m):
+        return send(held.at[m, pl.ds(rows, halo)], held.at[m, pl.ds(0, halo)], halo_send.at[0, m], halo_recv.at[0, m], place.right)
+
+    def halo_left(m):
+        return send(held.at[m, pl.ds(halo, halo)], held.at[m, pl.ds(rows + halo, halo)], halo_send.at[1, m], halo_recv.at[1, m], place.left)
+
+    at_start, at_end = place.s == 0, place.s == place.ns - 1
+
+    @pl.when(at_start)
+    def _():
+        held[:, 0:halo, :] = jnp.zeros((micro, halo, width), BF)
+
+    @pl.when(at_end)
+    def _():
+        held[:, rows + halo :, :] = jnp.zeros((micro, halo, width), BF)
+
+    tap_loads[0].wait()
+    inner_out = []
+    for m in range(micro):
+
+        def entry_step(i, m=m):
+            ns = span(i, tile_n)
+            total[m, :, ns] = mm(one[m], tap_w[0, :, ns], NN) + params[BE : BE + 1, ns]
+
+        for_each(width // tile_n, entry_step)
+        inner_out.append(store(total.at[m], inner_one.at[m]))
+
+        def norm_two(i, m=m):
+            rs = span(i, tile_r)
+            n, _ = normed(total[m, rs, :])
+            u = n * vec(G2) + vec(S2)
+            held[m, pl.ds(pl.multiple_of(halo + i * tile_r, tile_r), tile_r), :] = (u * phi(u)).astype(BF)
+
+        for_each(rows // tile_r, norm_two)
+
+        @pl.when(jnp.logical_not(at_end))
+        def _(m=m):
+            halo_right(m).start()
+
+        @pl.when(jnp.logical_not(at_start))
+        def _(m=m):
+            halo_left(m).start()
+
+        if m == 0:
+            tick(4)
+
+    tap_loads[1].wait()
+
+    def exit_step(i):
+        m, ns = i // (width // tile_n), span(lax.rem(i, width // tile_n), tile_n)
+        grad_three[m, :, ns] = mm(pulled[m], tap_w[1, :, ns], NN)
+
+    for_each(micro * (width // tile_n), exit_step)
+    tick(5)
+
+    for copy in inner_out:
+        copy.wait()
+
+    def conv_tap(i, first):
+        tap = TAP_ORDER[i - 2]
+        slot = i % 2
+        tap_loads[i].wait()
+        start = halo + (tap - KERNEL_TAPS // 2) * DILATION_STEP
+
+        def step(n):
+            m, ns = n // (width // tile_n), span(lax.rem(n, width // tile_n), tile_n)
+            got = mm(held[m, pl.ds(start, rows), :], tap_w[slot, :, ns], NN)
+            got = got * wide(keep(item, m, tap, rows, halo), tile_n)
+            if first:
+                total[m, :, ns] = got
+            else:
+                total[m, :, ns] += got
+
+        for_each(micro * (width // tile_n), step)
+
+    ext_out = []
+    for i in range(2, taps):
+        if i == 3:
+            for m in range(micro):
+
+                @pl.when(jnp.logical_not(at_start))
+                def _(m=m):
+                    halo_right(m).wait_recv()
+
+                @pl.when(jnp.logical_not(at_end))
+                def _(m=m):
+                    halo_left(m).wait_recv()
+
+                ext_out.append(store(held.at[m], ext_two.at[m]))
+        conv_tap(i, i == 2)
+        if i + 4 <= taps + 2:
+            tick(i + 4)
+
+    for copy in one_out + branch_out:
+        copy.wait()
+    for m in range(micro):
+
+        def norm_three(i, m=m):
+            rs = span(i, tile_r)
+            v = (total[m, rs, :] + vec(BC)).astype(BF).astype(F32)
+            n, inverse = normed(v)
+            u = n * vec(G3) + vec(S3)
+            big_phi = phi(u)
+            one[m, rs, :] = (u * big_phi).astype(BF)
+            t = grad_three[m, rs, :] * slope(u, big_phi)
+            sums[1] += fold(t * n)
+            sums[2] += fold(t)
+            grad = pull_back(t, n, inverse, vec(G3)).astype(BF)
+            pulled[m, rs, :] = grad
+            sums[0] += fold(grad.astype(F32))
+
+        for_each(rows // tile_r, norm_three)
+        store(one.at[m], act_three.at[m])
+        store(pulled.at[m], grad_two.at[m])
+
+    for copy in stores:
+        if not any(copy is done for done in one_out + branch_out + inner_out):
+            copy.wait()
+    for m in range(micro):
+
+        @pl.when(jnp.logical_not(at_end))
+        def _(m=m):
+            halo_right(m).wait_send()
+
+        @pl.when(jnp.logical_not(at_start))
+        def _(m=m):
+            halo_left(m).wait_send()
+
+    for copy in vec_copies:
+        copy.wait_send()
+    for copies in (z_copies, a_copies, c_copies):
+        for copy in copies.values():
+            copy.wait_send()
+    for copies in b_copies.values():
+        for copy in copies:
+            copy.wait_send()
+
+
+def forward(block_in, cotangent, lengths, weights, vectors, entry, conv, exit_t):
+    micro, rows, width = block_in.shape
+    halo = (KERNEL_TAPS // 2) * DILATION_STEP
+    taps = conv.shape[0] + 2
+    nz = lax.axis_size("fsdp")
+    extent = rows + 2 * halo
+    shape = jax.ShapeDtypeStruct
+    anywhere = pl.BlockSpec(memory_space=pl.ANY)
+    near = pl.BlockSpec(memory_space=pltpu.VMEM)
+    scalars = pl.BlockSpec(memory_space=pltpu.SMEM)
+    dma = pltpu.SemaphoreType.DMA
+    flops = 2 * micro * rows * width * width * taps
+    return pl.pallas_call(
+        forward_kernel,
+        out_shape=(
+            shape((taps, width, width), BF),
+            shape((micro, rows, width), BF),
+            shape((micro, rows, width), F32),
+            shape((micro, extent, width), BF),
+            shape((micro, rows, width), BF),
+            shape((micro, rows, width), BF),
+            shape((micro, rows, width), BF),
+            shape((VECTORS, width), F32),
+            shape((4, 8, width), F32),
+        ),
+        in_specs=[anywhere, anywhere, scalars, scalars, near, anywhere, anywhere, anywhere],
+        out_specs=(anywhere,) * 7 + (near, near),
+        scratch_shapes=[
+            pltpu.VMEM((micro, extent, width), BF),
+            pltpu.VMEM((micro, rows, width), F32),
+            pltpu.VMEM((micro, rows, width), F32),
+            pltpu.VMEM((2, width, width), BF),
+            pltpu.VMEM((micro, rows, width), BF),
+            pltpu.VMEM((micro, rows, width), BF),
+            pltpu.VMEM((micro, extent, LANES), jnp.int32),
+            pltpu.VMEM((micro, rows, LANES), F32),
+            pltpu.VMEM((nz,) + vectors.shape, BF),
+            dma((nz - 1,)),
+            dma((nz - 1,)),
+            dma((taps, nz - 1)),
+            dma((taps, nz - 1)),
+            dma((taps, nz - 1)),
+            dma((taps, nz - 1)),
+            dma((taps, nz - 1, 2)),
+            dma((taps, nz - 1, 2)),
+            dma((taps, nz - 1)),
+            dma((taps, nz - 1)),
+            dma((2, micro)),
+            dma((2, micro)),
+            dma((2, micro)),
+            dma((6 * micro,)),
+            dma((3, taps)),
+        ],
+        compiler_params=pltpu.CompilerParams(
+            collective_id=1, has_side_effects=True, vmem_limit_bytes=VMEM_MOST
+        ),
+        cost_estimate=pl.CostEstimate(flops=flops, bytes_accessed=80 << 20, transcendentals=0),
+        name="gather_and_forward",
+    )(block_in, cotangent, lengths, weights, vectors, entry, conv, exit_t)
+
+
+BACK_ORDER = (2, 1, 3, 0, 4)
+
+
+def backward_kernel(
+    block_in, cotangent, lengths, weights, params, sums_in, gathered, act_one, inner_one, ext_two, act_three, grad_two, grad_branch,
+    block_out, input_grad, shares, vec_out,
+    held, grads, total, buf, inner, item, scale, sums,
+    out_core, own, in_core, in_a, out_a, keep_a, in_b, out_b, keep_b, in_z, out_z, keep_z, final,
+    vec_part, vec_in,
+    core_send, core_recv, a_send, a_recv, b_send, b_recv, z_send, z_recv, f_own, f_send, f_recv, g_send, g_recv, h_send, h_recv,
+    halo_send, halo_recv, vec_send, vec_recv, load_sem, inner_sem, store_sem, credit,
+):
+    place = Place()
+    micro, rows, width = block_in.shape
+    halo = (KERNEL_TAPS // 2) * DILATION_STEP
+    z, c, q, x, y, nz = place.z, place.c, place.q, place.x, place.y, place.nz
+    taps, shard, _ = shares.shape
+    piece = shard // 4
+    half = width // 2
+    order = [1] + [2 + k for k in BACK_ORDER] + [0]
+    tile_n = 256
+    tile_m = 256
+    tile_r = 64
+    chunk = inner.shape[1]
+    across = width // tile_n
+    others = range(1, nz)
+    at_start, at_end = place.s == 0, place.s == place.ns - 1
+    low, high = pl.ds(0, micro * rows), pl.ds(micro * rows, micro * rows)
+    tap_rows = pl.ds(micro * rows, width)
+
+    def load(src, dst, n):
+        copy = pltpu.make_async_copy(src, dst, load_sem.at[n])
+        copy.start()
+        return copy
+
+    branch_in = [load(grad_branch.at[m], buf.at[pl.ds(m * rows, rows)], m) for m in range(micro)]
+    three_in = [load(act_three.at[m], buf.at[pl.ds((micro + m) * rows, rows)], micro + m) for m in range(micro)]
+    two_in = load(ext_two, held, 2 * micro)
+    grads_in = load(grad_two, grads.at[:, pl.ds(halo, rows)], 2 * micro + 1)
+    place.greet()
+
+    halo_right = send(grad_two.at[:, pl.ds(rows - halo, halo)], grads.at[:, pl.ds(0, halo)], halo_send.at[0], halo_recv.at[0], place.right)
+    halo_left = send(grad_two.at[:, pl.ds(0, halo)], grads.at[:, pl.ds(rows + halo, halo)], halo_send.at[1], halo_recv.at[1], place.left)
+
+    @pl.when(jnp.logical_not(at_end))
+    def _():
+        halo_right.start()
+
+    @pl.when(jnp.logical_not(at_start))
+    def _():
+        halo_left.start()
+
+    @pl.when(at_start)
+    def _():
+        grads[:, 0:halo, :] = jnp.zeros((micro, halo, width), BF)
+
+    @pl.when(at_end)
+    def _():
+        grads[:, rows + halo :, :] = jnp.zeros((micro, halo, width), BF)
+
+    find_items(place, lengths, weights, item, scale, micro, rows, halo)
+    sums[...] = jnp.zeros_like(sums)
+    for n, r in enumerate((BC, G3, S3, BX)):
+        sums[r] = sums_in[n]
+
+    def vec(r):
+        return params[r : r + 1, :]
+
+    my_cols = pl.ds(pl.multiple_of(c * half, LANES), half)
+    core_cols = pl.ds(pl.multiple_of(half - c * half, LANES), half)
+    sent = {}
+
+    def axes(i):
+        if i % 2 == 0:
+            return x, y, place.px, place.py
+        return y, x, place.py, place.px
+
+    def block_rows(i, zz, other, mine):
+        step_mine, step_other = (piece, 2 * piece) if i % 2 == 0 else (2 * piece, piece)
+        return pl.ds(pl.multiple_of(zz * shard + other * step_other + mine * step_mine, 16), piece)
+
+    def stage_core(i):
+        copy = send(out_core, in_core, core_send.at[i], core_recv.at[i], place.core)
+        if i > 0:
+            pl.semaphore_wait(credit, 1)
+        copy.start()
+        sent["core", i] = copy
+
+    def stage_a(i):
+        mine, _, peer, _ = axes(i)
+        slot = i % 2
+        sent["core", i].wait_recv()
+        if i >= 2:
+            sent["a", i - 2].wait_send()
+
+        def step(n):
+            zz, other = n // 2, lax.rem(n, 2)
+            kept = block_rows(i, zz, other, mine)
+            gone = block_rows(i, zz, other, 1 - mine)
+            out_a[slot, n] = (own[gone, :].astype(F32) + in_core[gone, :].astype(F32)).astype(BF)
+            keep_a[slot, n] = (own[kept, :].astype(F32) + in_core[kept, :].astype(F32)).astype(keep_a.dtype)
+
+        for_each(2 * nz, step)
+        copy = send(out_a.at[slot], in_a.at[i], a_send.at[i], a_recv.at[i], peer)
+        copy.start()
+        sent["a", i] = copy
+        if i < taps - 1:
+            pl.semaphore_signal(credit, inc=1, device_id=place.core, device_id_type=MESH)
+
+    def stage_b(i):
+        _, mine, _, peer = axes(i)
+        slot = i % 2
+        sent["a", i].wait_recv()
+        if i >= 2:
+            sent["b", i - 2].wait_send()
+
+        def step(zz):
+            kept, gone = 2 * zz + mine, 2 * zz + 1 - mine
+            out_b[slot, zz] = (keep_a[slot, gone].astype(F32) + in_a[i, gone].astype(F32)).astype(BF)
+            keep_b[slot, zz] = keep_a[slot, kept].astype(F32) + in_a[i, kept].astype(F32)
+
+        for_each(nz, step)
+        copy = send(out_b.at[slot], in_b.at[i], b_send.at[i], b_recv.at[i], peer)
+        copy.start()
+        sent["b", i] = copy
+
+    def stage_z(i):
+        slot = i % 2
+        sent["b", i].wait_recv()
+        for j in range(nz):
+            if j > 0 and i >= 2:
+                sent["z", i - 2, j].wait_send()
+            zz = place.up(j)
+            value = keep_b[slot, zz] + in_b[i, zz].astype(F32)
+            if j == 0:
+                keep_z[slot] = value
+                continue
+            out_z[slot, j - 1] = value.astype(BF)
+            copy = send(out_z.at[slot, j - 1], in_z.at[i, j - 1], z_send.at[i, j - 1], z_recv.at[i, j - 1], place.above(j))
+            copy.start()
+            sent["z", i, j] = copy
+
+    def share_at(i, first, count):
+        return shares.at[order[i], pl.ds(pl.multiple_of(first * piece, 16), count * piece), my_cols]
+
+    def stage_final(i):
+        slot = i % 2
+        value = keep_z[slot]
+        for j in others:
+            sent["z", i, j].wait_recv()
+            value = value + in_z[i, j - 1].astype(F32)
+        if i >= 2:
+            sent["f", i - 2].wait_send()
+        final[slot] = value.astype(BF)
+        here = pltpu.make_async_copy(final.at[slot], share_at(i, q, 1), f_own.at[i])
+        here.start()
+        copy = send(final.at[slot], share_at(i, q, 1), f_send.at[i], f_recv.at[i], axes(i)[2])
+        copy.start()
+        sent["f", i] = copy
+        sent["own", i] = here
+
+    def stage_g(i):
+        sent["own", i].wait()
+        sent["f", i].wait_recv()
+        if i % 2 == 0:
+            blocks = [share_at(i, 2 * y, 2)]
+        else:
+            blocks = [share_at(i, x, 1), share_at(i, x + 2, 1)]
+        for n, block in enumerate(blocks):
+            copy = send(block, block, g_send.at[i, n], g_recv.at[i, n], axes(i)[3])
+            copy.start()
+            sent["g", i, n] = copy
+
+    def stage_h(i):
+        for n in range(1 + i % 2):
+            sent["g", i, n].wait_recv()
+        block = share_at(i, 0, 4)
+        copy = send(block, block, h_send.at[i], h_recv.at[i], place.core)
+        copy.start()
+        sent["h", i] = copy
+
+    def tick(i):
+        for back, stage in ((4, stage_h), (3, stage_g), (2, stage_final), (1, stage_z), (0, stage_b)):
+            if 0 <= i - back < taps:
+                stage(i - back)
+
+    def weight_grad(i, product):
+        if i > 0:
+            sent["core", i - 1].wait_send()
+
+        def far(n):
+            ms = span(n, tile_m)
+            out_core[ms, :] = product(ms, core_cols).astype(BF)
+
+        for_each(width // tile_m, far)
+        stage_core(i)
+
+        def near(n):
+            ms = span(n, tile_m)
+            own[ms, :] = product(ms, my_cols).astype(own.dtype)
+
+        for_each(width // tile_m, near)
+        stage_a(i)
+
+    for copy in branch_in + three_in:
+        copy.wait()
+    weight_grad(0, lambda ms, ns: mm(buf[low, ms], buf[high, ns], TN))
+
+    def load_tap(k):
+        return load(gathered.at[2 + k], buf.at[tap_rows], 2 * micro + 2)
+
+    tap_in = load_tap(BACK_ORDER[0])
+    two_in.wait()
+    grads_in.wait()
+
+    def back_tap(n, k, first):
+        start = halo - (k - KERNEL_TAPS // 2) * DILATION_STEP
+
+        def step(i):
+            m, j = i // across, lax.rem(i, across)
+            ns = span(j, tile_n)
+            rs = pl.ds(pl.multiple_of(micro * rows + j * tile_n, tile_n), tile_n)
+            got = mm(grads[m, pl.ds(start, rows), :], buf[rs, :], NT)
+            got = got * wide(keep(item, m, KERNEL_TAPS - 1 - k, rows, halo), tile_n)
+            if first:
+                total[m, :, ns] = got
+            else:
+                total[m, :, ns] += got
+
+        for_each(micro * across, step)
+
+    for n, k in enumerate(BACK_ORDER):
+
+        def masked(i, k=k):
+            m, r = i // (rows // 128), lax.rem(i, rows // 128)
+            first = pl.multiple_of(halo + r * 128, 128)
+            tap_first = pl.multiple_of(first + (k - KERNEL_TAPS // 2) * DILATION_STEP, 128)
+            mine = item[m, pl.ds(first, 128)]
+            mask = jnp.where((mine == item[m, pl.ds(tap_first, 128)]) & (mine >= 0), 1.0, 0.0)
+            value = grads[m, pl.ds(first, 128), :].astype(F32) * wide(mask, width)
+            buf[span(i, 128), :] = value.astype(BF)
+
+        for_each(micro * rows // 128, masked)
+        start = halo + (k - KERNEL_TAPS // 2) * DILATION_STEP
+
+        def product(ms, ns, start=start):
+            got = None
+            for m in range(micro):
+                part = mm(held[m, pl.ds(start, rows), ms], buf[pl.ds(m * rows, rows), ns], TN)
+                got = part if got is None else got + part
+            return got
+
+        weight_grad(n + 1, product)
+        if n == 1:
+
+            @pl.when(jnp.logical_not(at_start))
+            def _():
+                halo_right.wait_recv()
+
+            @pl.when(jnp.logical_not(at_end))
+            def _():
+                halo_left.wait_recv()
+
+        tap_in.wait()
+        back_tap(n, k, n == 0)
+        if n + 1 < len(BACK_ORDER):
+            tap_in = load_tap(BACK_ORDER[n + 1])
+        tick(n)
+
+    entry_in = load(gathered.at[0], buf.at[tap_rows], 2 * micro + 2)
+    one_in = [load(act_one.at[m], held.at[m, pl.ds(0, rows)], m) for m in range(micro)]
+    block_load = [load(block_in.at[m], held.at[m, pl.ds(rows, rows)], micro + m) for m in range(micro)]
+    pull_in = load(cotangent, grads.at[:, pl.ds(0, rows)], 2 * micro)
+    chunks = micro * rows // chunk
+    per_block = rows // chunk
+
+    def fetch(n):
+        m, r = n // per_block, lax.rem(n, per_block)
+        slot = lax.rem(n, 2)
+        return pltpu.make_async_copy(inner_one.at[m, span(r, chunk)], inner.at[slot], inner_sem.at[slot])
+
+    fetch(0).start()
+
+    def norm_two(n):
+        m, r = n // per_block, lax.rem(n, per_block)
+        slot = lax.rem(n, 2)
+
+        @pl.when(n + 1 < chunks)
+        def _():
+            fetch(n + 1).start()
+
+        fetch(n).wait()
+        for part in range(chunk // tile_r):
+            rs = pl.ds(pl.multiple_of(r * chunk + part * tile_r, tile_r), tile_r)
+            norm, inverse = normed(inner[slot, part * tile_r : (part + 1) * tile_r, :])
+            u = norm * vec(G2) + vec(S2)
+            t = total[m, rs, :] * slope(u, phi(u))
+            sums[G2] += fold(t * norm)
+            sums[S2] += fold(t)
+            grad = pull_back(t, norm, inverse, vec(G2)).astype(BF)
+            buf[pl.ds(pl.multiple_of(n * chunk + part * tile_r, tile_r), tile_r), :] = grad
+            sums[BE] += fold(grad.astype(F32))
+
+    for_each(chunks, norm_two)
+    tick(5)
+
+    for copy in one_in:
+        copy.wait()
+
+    def entry_product(ms, ns):
+        got = None
+        for m in range(micro):
+            part = mm(held[m, pl.ds(0, rows), ms], buf[pl.ds(m * rows, rows), ns], TN)
+            got = part if got is None else got + part
+        return got
+
+    weight_grad(taps - 1, entry_product)
+    three_again = [load(act_three.at[m], held.at[m, pl.ds(0, rows)], m) for m in range(micro)]
+
+    entry_in.wait()
+
+    def entry_step(i):
+        m, j = i // across, lax.rem(i, across)
+        rs = pl.ds(pl.multiple_of(micro * rows + j * tile_n, tile_n), tile_n)
+        total[m, :, span(j, tile_n)] = mm(buf[span(m, rows), :], buf[rs, :], NT)
+
+    for_each(micro * across, entry_step)
+    exit_in = load(gathered.at[1], buf.at[tap_rows], 2 * micro + 2)
+    tick(6)
+    pull_in.wait()
+    stores = []
+    for m in range(micro):
+        block_load[m].wait()
+
+        def norm_one(i, m=m):
+            rs = span(i, tile_r)
+            norm, inverse = normed(held[m, pl.ds(pl.multiple_of(rows + i * tile_r, tile_r), tile_r), :].astype(F32))
+            u = norm * vec(G1) + vec(S1)
+            t = total[m, rs, :] * slope(u, phi(u))
+            sums[G1] += fold(t * norm)
+            sums[S1] += fold(t)
+            grad = pull_back(t, norm, inverse, vec(G1))
+            pulled = grads[m, rs, :].astype(F32) * wide(scale[m, rs, :], width)
+            grads[m, rs, :] = (pulled + grad).astype(BF)
+
+        for_each(rows // tile_r, norm_one)
+        copy = pltpu.make_async_copy(grads.at[m, pl.ds(0, rows)], input_grad.at[m], store_sem.at[0, m])
+        copy.start()
+        stores.append(copy)
+    tick(7)
+
+    vec_part[0] = jnp.zeros_like(vec_part[0])
+    for r in range(sums.shape[0]):
+        vec_part[0, r : r + 1, :] = jnp.sum(sums[r], axis=0, keepdims=True)
+
+    def vec_stage(n, peer):
+        copy = send(vec_part.at[n], vec_in.at[n], vec_send.at[n], vec_recv.at[n], peer)
+        copy.start()
+        sent["v", n] = copy
+
+    def vec_add(n):
+        sent["v", n].wait_recv()
+        vec_part[n + 1] = vec_part[n] + vec_in[n]
+
+    vec_stage(0, place.core)
+
+    exit_in.wait()
+    for m in range(micro):
+        three_again[m].wait()
+
+        def exit_step(j, m=m):
+            ns = span(j, tile_n)
+            rs = pl.ds(pl.multiple_of(micro * rows + j * tile_n, tile_n), tile_n)
+            got = mm(held[m, pl.ds(0, rows), :], buf[rs, :], NT) + params[BX : BX + 1, ns]
+            out = held[m, pl.ds(rows, rows), ns].astype(F32) + got
+            held[m, pl.ds(rows, rows), ns] = out.astype(BF)
+
+        for_each(across, exit_step)
+        copy = pltpu.make_async_copy(held.at[m, pl.ds(rows, rows)], block_out.at[m], store_sem.at[1, m])
+        copy.start()
+        stores.append(copy)
+        vec_add(m)
+        if m == 0:
+            vec_stage(1, place.px)
+        elif m == 1:
+            vec_stage(2, place.py)
+    tick(8)
+    for j in others:
+        copy = send(vec_part.at[3], vec_in.at[2 + j], vec_send.at[2 + j], vec_recv.at[2 + j], place.above(j))
+        copy.start()
+        sent["v", 2 + j] = copy
+    tick(9)
+    value = vec_part[3]
+    for j in others:
+        sent["v", 2 + j].wait_recv()
+        value = value + vec_in[2 + j]
+    vec_out[...] = value
+    tick(10)
+    for i in range(taps):
+        sent["h", i].wait_recv()
+    for copy in stores:
+        copy.wait()
+
+    @pl.when(jnp.logical_not(at_end))
+    def _():
+        halo_right.wait_send()
+
+    @pl.when(jnp.logical_not(at_start))
+    def _():
+        halo_left.wait_send()
+
+    sent["core", taps - 1].wait_send()
+    for key, copy in sent.items():
+        if key[0] in ("a", "b", "z", "f") and key[1] >= taps - 2 or key[0] in ("g", "h", "v"):
+            copy.wait_send()
+
+
+def backward(block_in, cotangent, lengths, weights, shard, kept):
+    gathered, act_one, inner_one, ext_two, act_three, grad_two, grad_branch, params, sums = kept
+    micro, rows, width = block_in.shape
+    halo = (KERNEL_TAPS // 2) * DILATION_STEP
+    taps = gathered.shape[0]
+    nz = lax.axis_size("fsdp")
+    extent = rows + 2 * halo
+    piece = shard // 4
+    half = width // 2
+    shape = jax.ShapeDtypeStruct
+    anywhere = pl.BlockSpec(memory_space=pl.ANY)
+    near = pl.BlockSpec(memory_space=pltpu.VMEM)
+    scalars = pl.BlockSpec(memory_space=pltpu.SMEM)
+    dma = pltpu.SemaphoreType.DMA
+    vmem = pltpu.VMEM
+    flops = 2 * micro * rows * width * width * (2 * taps)
+    return pl.pallas_call(
+        backward_kernel,
+        out_shape=(
+            shape((micro, rows, width), BF),
+            shape((micro, rows, width), BF),
+            shape((taps, shard, width), BF),
+            shape((VECTORS, width), F32),
+        ),
+        in_specs=[anywhere, anywhere, scalars, scalars, near, near] + [anywhere] * 7,
+        out_specs=(anywhere, anywhere, anywhere, near),
+        scratch_shapes=[
+            vmem((micro, extent, width), BF),
+            vmem((micro, extent, width), BF),
+            vmem((micro, rows, width), F32),
+            vmem((2 * micro * rows, width), BF),
+            vmem((2, 128, width), F32),
+            vmem((micro, extent, LANES), jnp.int32),
+            vmem((micro, rows, LANES), F32),
+            vmem((9, 8, width), F32),
+            vmem((width, half), BF),
+            vmem((width, half), BF),
+            vmem((width, half), BF),
+            vmem((taps, 2 * nz, piece, half), BF),
+            vmem((2, 2 * nz, piece, half), BF),
+            vmem((2, 2 * nz, piece, half), BF),
+            vmem((taps, nz, piece, half), BF),
+            vmem((2, nz, piece, half), BF),
+            vmem((2, nz, piece, half), F32),
+            vmem((taps, nz - 1, piece, half), BF),
+            vmem((2, nz - 1, piece, half), BF),
+            vmem((2, piece, half), F32),
+            vmem((2, piece, half), BF),
+            vmem((4, VECTORS, width), F32),
+            vmem((2 + nz, VECTORS, width), F32),
+            dma((taps,)),
+            dma((taps,)),
+            dma((taps,)),
+            dma((taps,)),
+            dma((taps,)),
+            dma((taps,)),
+            dma((taps, nz - 1)),
+            dma((taps, nz - 1)),
+            dma((taps,)),
+            dma((taps,)),
+            dma((taps,)),
+            dma((taps, 2)),
+            dma((taps, 2)),
+            dma((taps,)),
+            dma((taps,)),
+            dma((2,)),
+            dma((2,)),
+            dma((2 + nz,)),
+            dma((2 + nz,)),
+            dma((2 * micro + 3,)),
+            dma((2,)),
+            dma((2, micro)),
+            pltpu.SemaphoreType.REGULAR,
+        ],
+        compiler_params=pltpu.CompilerParams(
+            collective_id=2, has_side_effects=True, vmem_limit_bytes=VMEM_MOST
+        ),
+        cost_estimate=pl.CostEstimate(flops=flops, bytes_accessed=80 << 20, transcendentals=0),
+        name="backward_and_reduce",
+    )(block_in, cotangent, lengths, weights, params, sums, gathered, act_one, inner_one, ext_two, act_three, grad_two, grad_branch)
+
+
+def kernels_on_device(
+    block_in,
+    cotangent,
+    lengths,
+    item_weights,
+    first_gain,
+    first_shift,
+    entry_weight,
+    entry_bias,
+    middle_gain,
+    middle_shift,
+    conv_weight,
+    conv_bias,
+    final_gain,
+    final_shift,
+    exit_weight,
+    exit_bias,
+):
+    shard = entry_weight.shape[0]
+    rows = [
+        first_gain,
+        first_shift,
+        entry_bias,
+        middle_gain,
+        middle_shift,
+        conv_bias,
+        final_gain,
+        final_shift,
+        exit_bias,
+    ]
+    padded = -(-shard // LANES) * LANES
+    vectors = jnp.pad(jnp.stack(rows), ((0, VECTORS - len(rows)), (0, padded - shard)))
+    own_lengths, own_weights = lengths[:, 0], item_weights[:, 0]
+    kept = forward(
+        block_in, cotangent, own_lengths, own_weights, vectors, entry_weight, conv_weight, exit_weight.T
+    )
+    outputs, input_grads, shares, sums = backward(
+        block_in, cotangent, own_lengths, own_weights, shard, kept
+    )
+    own_sums = lax.dynamic_slice_in_dim(sums, lax.axis_index("fsdp") * shard, shard, axis=1)
+    vec = [own_sums[r] for r in range(len(rows))]
+    return (
+        outputs,
+        input_grads,
+        vec[G1],
+        vec[S1],
+        shares[0].astype(F32),
+        vec[BE],
+        vec[G2],
+        vec[S2],
+        shares[2:].astype(F32),
+        vec[BC],
+        vec[G3],
+        vec[S3],
+        shares[1].astype(F32).T,
+        vec[BX],
+    )
+
+
+def fits(mesh):
+    return mesh.shape["seq"] == 8
 
 
 def norm_act(values, scale_vec, shift_vec):
@@ -32,7 +1107,10 @@
 
 
 def items_at(residue_position, item_lengths, stream_len):
-    ends = jnp.cumsum(item_lengths)
+    item_places = jnp.arange(item_lengths.shape[0], dtype=jnp.int32)
+    ends = jnp.sum(
+        jnp.where(item_places[:, None] <= item_places[None, :], item_lengths[:, None], 0), axis=0
+    )
     inside = (residue_position >= 0) & (residue_position < stream_len)
     seg_all = jnp.sum((residue_position[:, None] >= ends[None, :]).astype(jnp.int32), axis=1)
     return jnp.where(inside, seg_all, -1)
@@ -328,6 +1406,7 @@
         P(None, "fsdp"),
         P("fsdp"),
     )
+    body = kernels_on_device if fits(mesh) else on_device
     return jax.shard_map(
-        on_device, mesh=mesh, in_specs=in_specs, out_specs=out_specs, check_vma=False
+        body, mesh=mesh, in_specs=in_specs, out_specs=out_specs, check_vma=False
     )

time: 1610 us -> 462 us (0.29)
  waiting for transfers between devices: 914 us -> 0 us
  Pallas kernels: 0 us -> 435 us
  matrix products: 259 us -> 0 us
  other arithmetic: 163 us -> 9.59 us
  blocking collectives: 104 us -> 0 us
  local copies, waits for them, and re-layouts: 97.4 us -> 16.2 us
  starting transfers between devices: 45.8 us -> 0 us
  between operations: 18.3 us -> 0.67 us
    reduce_scatter x3 -> x0, waiting for transfers between devices: 525 us -> none  [the longest x1 525 us: on_device(): lax.psum_scatter(totals[6], 'fsdp', scatter_dimension=1, tiled=True)]
    pallas_call x0 -> x2, Pallas kernels: none -> 435 us  [the longest x1 226 us: backward(): pl.pallas_call(backward_kernel, out_shape=(shape((micro, rows, width), BF...]
    dot_general x27 -> x0, matrix products: 259 us -> none  [the longest x9 113 us: column_product(): lax.dot_general(left, right, (((0,), (0,)), ((), ())), preferred_element_...]
    all_gather x3 -> x0, waiting for transfers between devices: 184 us -> none  [the longest x1 169 us: on_device(): lax.all_gather(conv_weight, 'fsdp', axis=1, tiled=True)]
    all_to_all x11 -> x0, waiting for transfers between devices: 105 us -> none  [the longest x2 42.3 us: on_device(): lax.all_to_all(dealt_back.reshape(sequence_count, row_count // sequence_c...]
    psum x1 -> x0, waiting for transfers between devices: 97.9 us -> none  [on_device(): lax.psum((shares[0], shares[1], shares[2], shares[3], shares[4], shares[5...]
    reduce_sum x26 -> x0, other arithmetic: 47.9 us -> none  [the longest x3 14.3 us: norm_act(): centred = values - row_mean]
    all_to_all x11 -> x0, starting transfers between devices: 44.5 us -> none  [the longest x3 12.7 us: on_device(): lax.all_to_all(dealt_out.reshape(sequence_count, row_count // sequence_co...]
  transfers between devices with their start and end apart: 18 -> 0, of which waited for: 11 -> 0; matrix products, arithmetic and copies ran while one was open for 29% -> 0% of each run, Pallas kernels for 0% -> 0%
where the time goes in v1:
time: 462 us
  Pallas kernels  435 us (94%)
  local copies, waits for them, and re-layouts  16.2 us (4%)
  other arithmetic  9.59 us (2%)
    pallas_call x1, Pallas kernels, backward(): pl.pallas_call(backward_kernel, out_shape=(shape((micro, rows, width), BF...  226 us
    pallas_call x1, Pallas kernels, forward(): pl.pallas_call(forward_kernel, out_shape=(shape((taps, width, width), BF)...  209 us

profile of v1, /device:TPU:0, one launch (start us, length us, event | category | flops | bytes accessed | tf_op | source)
XLA Modules:
  0.0 461.5 jit_solution(9326976048326059833)
XLA Ops:
  0.6 1.3 copy_bitcast_fusion
  1.9 0.7 stack.30
  2.6 0.7 stack.31
  3.3 0.7 stack.32
  4.0 0.7 stack.33
  4.7 0.7 stack.34
  5.3 0.7 stack.35
  6.0 0.7 stack.36
  6.7 0.7 stack.37
  7.4 0.7 stack.38
  8.1 0.1 stack.39
  8.1 0.6 pad.4.vectors
  8.7 209.2 %gather_and_forward.1 = (bf16[7,1280,1280]{2,1,0:T(8,128)(2,1)}, bf16[3,512,1280]{2,1,0:T(8,128)(2,1)}, f32[3,512,1280]{2,1,0:T(8,128)}, bf16[3,1024,1280]{2,1,0...) custom-call(bf16[3,512,1280]{2,1,0:T(8,128)(2,1)} %block_in.3, ...), custom_call_target="tpu_custom_call" | custom-call | flops 35232153600 | bytes 83886080 | tf_op jit(solution)/shard_map/gather_and_forward/pallas_call | solution.py:477
  217.9 225.9 %backward_and_reduce.1 = (bf16[3,512,1280]{2,1,0:T(8,128)(2,1)}, bf16[3,512,1280]{2,1,0:T(8,128)(2,1)}, bf16[7,320,1280]{2,1,0:T(8,128)(2,1)}, f32[16,1280]{1,0:T(8,128)}) custom-call(bf16[3,512,1280]{2,1,0:T(8,128)(2,1)} %block_in.3, bf16[3,512,1280]{2,1,0:T(8,128)(2,1)} %cotangent.3, s32[3,8]{1,0:T(4,128)} %get-tuple-element.52.lengths, ...), custom_call_target="tpu_custom_call" | custom-call | flops 70464307200 | bytes 83886080 | tf_op jit(solution)/shard_map/backward_and_reduce/pallas_call | solution.py:959
  443.9 6.2 %slice_convert_fusion = f32[5,320,1280]{2,1,0:T(8,128)} fusion(bf16[7,320,1280]{2,1,0:T(8,128)(2,1)} %get-tuple-element.39), kind=kLoop, calls=%fused_computation | loop fusion | flops 2048000 | bytes 12288000 | tf_op jit(solution)/shard_map/convert_element_type | solution.py:1075
  450.1 3.3 convert_bitcast_fusion
  453.5 1.7 dynamic-slice_reduce_fusion
  455.2 0.0 copy-start
  455.2 4.4 copy.36
  459.6 0.0 copy-done
  459.6 1.9 copy.37
Async XLA Ops:
  455.2 4.4 copy-start
